TPU v7x, 128 devices: a whole 4x4x4 slice. The times are simulated.
128 devices in a mesh: depth: 8 (over z, y_lo), height: 16 (over x, y_hi, core).
Axes of the slice: x: 4, y: 4 (y_hi: 2, y_lo: 2; y = y_hi * 2 + y_lo), z: 4, core: 2. Of those that a mesh axis runs over, the one named last changes fastest.
Arguments:
- volume: bfloat16 [32, 32, 128, 128], P(None, 'depth', 'height'), may hold values from -6 to 6
- filters_three: bfloat16 [27, 64, 32], replicated, may hold values from -0.21875 to 0.21875
- filters_four: bfloat16 [27, 128, 64], P(None, 'height'), may hold values from -0.15625 to 0.15625
- cotangent: bfloat16 [128, 16, 64, 64], P(None, 'depth', 'height'), may hold values from -6 to 6
Outputs:
- grad_volume: bfloat16 [32, 32, 128, 128], P(None, 'depth', 'height')
- grad_three: float32 [27, 64, 32], replicated
- grad_four: float32 [27, 128, 64], P(None, 'height')
All inputs are finite; a program needn't handle non-finite values.
Results may differ from a plain program's by a relative error of at most 0.023.
Values may be sent and summed in bfloat16 or wider, within the bound.
A program may use at most 256 MiB of HBM per device.

v0:
```python
import math
import jax
import jax.numpy as jnp
from jax import lax
from jax.sharding import PartitionSpec as P

TANH_SCALE = 0.7978845608028654
CUBIC_TERM = 0.044715


def extended_2(x, sides, width):
    for axis, dim in sides:
        size, length = (lax.axis_size(axis), x.shape[dim])
        up = [(i, (i + 1) % size) for i in range(size - 1)]
        down = [(j, i) for i, j in up]
        last = lax.slice_in_dim(x, length - width, length, axis=dim)
        first = lax.slice_in_dim(x, 0, width, axis=dim)
        before = lax.ppermute(last, axis, up)
        after = lax.ppermute(first, axis, down)
        x = jnp.concatenate([before, x, after], axis=dim)
    return x


def gelu_value(values_in):
    inner = jnp.tanh(TANH_SCALE * (values_in + CUBIC_TERM * values_in * values_in * values_in))
    return 0.5 * values_in * (1.0 + inner)


def gelu_slope(values_in):
    inner = jnp.tanh(TANH_SCALE * (values_in + CUBIC_TERM * values_in * values_in * values_in))
    return 0.5 * (1.0 + inner) + 0.5 * values_in * (1.0 - inner * inner) * TANH_SCALE * (
        1.0 + 3.0 * CUBIC_TERM * values_in * values_in
    )


def pad_width(values_in):
    return jnp.pad(values_in, ((0, 0), (0, 0), (0, 0), (1, 1)))


def forward_taps(padded, weights, depth_cells, height_cells, width_cells):
    running = jnp.zeros((weights.shape[1], depth_cells, height_cells, width_cells), jnp.float32)
    for first in range(3):
        for second in range(3):
            for third in range(3):
                window_piece = padded[
                    :,
                    first : first + depth_cells,
                    second : second + height_cells,
                    third : third + width_cells,
                ]
                running = running + jnp.einsum(
                    "oi,idhw->odhw",
                    weights[9 * first + 3 * second + third],
                    window_piece,
                    preferred_element_type=jnp.float32,
                )
    return running


def transpose_taps(padded, weights, depth_cells, height_cells, width_cells):
    running = jnp.zeros((weights.shape[2], depth_cells, height_cells, width_cells), jnp.float32)
    for first in range(3):
        for second in range(3):
            for third in range(3):
                window_piece = padded[
                    :,
                    2 - first : 2 - first + depth_cells,
                    2 - second : 2 - second + height_cells,
                    2 - third : 2 - third + width_cells,
                ]
                running = running + jnp.einsum(
                    "oi,odhw->idhw",
                    weights[9 * first + 3 * second + third],
                    window_piece,
                    preferred_element_type=jnp.float32,
                )
    return running


def weight_taps(delta, padded, depth_cells, height_cells, width_cells):
    collected = []
    for first in range(3):
        for second in range(3):
            for third in range(3):
                window_piece = padded[
                    :,
                    first : first + depth_cells,
                    second : second + height_cells,
                    third : third + width_cells,
                ]
                collected.append(
                    jnp.einsum(
                        "odhw,idhw->oi", delta, window_piece, preferred_element_type=jnp.float32
                    )
                )
    return jnp.stack(collected, axis=0)


def shards(volume, filters_three, filters_four, cotangent):
    channels_in, depth_cells, height_cells, width_cells = volume.shape
    depth_count = lax.axis_size("depth")
    height_count = lax.axis_size("height")
    scale_three = 1.0 / math.sqrt(
        depth_cells * depth_count * height_cells * height_count * width_cells
    )
    scale_four = 1.0 / math.sqrt(
        depth_cells * depth_count // 2 * (height_cells * height_count // 2) * (width_cells // 2)
    )
    half_depth = depth_cells // 2
    half_height = height_cells // 2
    half_width = width_cells // 2
    extended = extended_2(volume, (("depth", 1), ("height", 2)), 1)
    padded = pad_width(extended)
    act_three = forward_taps(padded, filters_three, depth_cells, height_cells, width_cells)
    channels_mid = act_three.shape[0]
    hidden = gelu_value(act_three).reshape(
        channels_mid, half_depth, 2, half_height, 2, half_width, 2
    )
    pooled = (jnp.sum(hidden, axis=(2, 4, 6)) * 0.125).astype(jnp.bfloat16)
    full_bank = lax.all_gather(filters_four, "height", axis=1, tiled=True)
    rimmed = extended_2(pooled, (("depth", 1), ("height", 2)), 1)
    pooled_pad = pad_width(rimmed)
    act_four = forward_taps(pooled_pad, full_bank, half_depth, half_height, half_width)
    delta_four = (cotangent.astype(jnp.float32) * gelu_slope(act_four)).astype(jnp.bfloat16)
    partial_four = weight_taps(delta_four, pooled_pad, half_depth, half_height, half_width)
    depth_summed = lax.psum(partial_four.astype(jnp.bfloat16), "depth")
    grad_four = (
        lax.psum_scatter(depth_summed, "height", scatter_dimension=1, tiled=True).astype(
            jnp.float32
        )
        * scale_four
    )
    delta_rim = extended_2(delta_four, (("depth", 1), ("height", 2)), 1)
    back_pooled = transpose_taps(
        pad_width(delta_rim), full_bank, half_depth, half_height, half_width
    )
    spread = (
        jnp.repeat(jnp.repeat(jnp.repeat(back_pooled, 2, axis=1), 2, axis=2), 2, axis=3) * 0.125
    )
    delta_three = (spread * gelu_slope(act_three)).astype(jnp.bfloat16)
    partial_three = weight_taps(delta_three, padded, depth_cells, height_cells, width_cells)
    grad_three = lax.psum(partial_three, ("depth", "height")) * scale_three
    delta_extended = extended_2(delta_three, (("depth", 1), ("height", 2)), 1)
    grad_volume = transpose_taps(
        pad_width(delta_extended), filters_three, depth_cells, height_cells, width_cells
    ).astype(jnp.bfloat16)
    return (grad_volume, grad_three, grad_four)


def solution(mesh):
    in_specs = (
        P(None, "depth", "height", None),
        P(),
        P(None, "height", None),
        P(None, "depth", "height", None),
    )
    out_specs = (P(None, "depth", "height", None), P(), P(None, "height", None))
    return jax.shard_map(shards, mesh=mesh, in_specs=in_specs, out_specs=out_specs, check_vma=False)
```

profile of v0, /device:TPU:6, one launch (start us, length us, event | category | flops | bytes accessed | tf_op | source)
XLA Modules:
  0.0 348.1 jit_solution(2866375884435285282)
XLA Ops:
  8.1 0.9 fusion.559
  9.0 3.5 %collective-permute-start = (bf16[32,1,8,128]{3,0,2,1:T(8,128)(2,1)S(1)}, bf16[32,1,8,128]{3,0,2,1:T(8,128)(2,1)S(1)}, u32[]{:S(2)}, u32[]{:S(2)}) collective-permute-start(bf16[32,1,8,128]{3,0,2,1:T(8,128)(2,1)S(1)} %copy.321), channel_id=1, source_target_pairs={{0,16},{16,32},{32,48},{48,64},{64,80},{80,96},{96,112},{1,17},{17... | collective-permute-start | bytes 196616 | tf_op jit(solution)/shard_map/ppermute | solution.py:18
  12.5 1.3 collective-permute-start.1
  13.8 0.6 collective-permute-done
  14.4 1.2 constant_dynamic-update-slice_fusion.6
  15.6 3.1 collective-permute-done.1
  18.8 1.9 collective-permute-start.2
  20.7 6.0 %collective-permute-start.3 = (bf16[32,6,1,128]{3,0,2,1:T(8,128)(2,1)S(1)}, bf16[32,6,1,128]{3,0,2,1:T(8,128)(2,1)S(1)}, u32[]{:S(2)}, u32[]{:S(2)}) collective-permute-start(bf16[32,6,1,128]{3,0,2,1:T(8,128)(2,1)S(1)} %get-tuple-element.19), channel_id=1, source_target_pairs={{1,0},{2,1},{3,2},{4,3},{5,4},{6,5},{7,6},{8,7},{9,8},{10,9},{11,1... | collective-permute-start | bytes 147464 | tf_op jit(solution)/shard_map/ppermute | solution.py:19
  27.1 1.4 collective-permute-done.3
  28.5 0.5 fusion.212
  29.3 0.4 fusion.320
  30.0 0.4 fusion.314
  30.7 0.4 fusion.308
  31.1 0.4 convolution_bitcast_fusion.10
  32.2 0.4 convolution_bitcast_fusion.8
  32.9 0.4 convolution_bitcast_fusion.4
  33.7 0.4 convolution_bitcast_fusion.6
  34.7 0.4 convolution_add_fusion.4
  36.9 0.4 fusion.22
  37.3 0.7 fusion.27
  38.3 2.0 add_multiply_fusion
  40.4 1.8 copy.91
  42.2 2.4 reduce_sum.9
  44.6 1.0 multiply_convert_fusion
  45.6 4.6 %collective-permute-start.4 = (bf16[64,1,4,64]{0,3,2,1:T(8,128)(2,1)S(1)}, bf16[64,1,4,64]{0,3,2,1:T(8,128)(2,1)S(1)}, u32[]{:S(2)}, u32[]{:S(2)}) collective-permute-start(bf16[64,1,4,64]{0,3,2,1:T(8,128)(2,1)S(1)} %get-tuple-element.33), channel_id=1, source_target_pairs={{0,16},{16,32},{32,48},{48,64},{64,80},{80,96},{96,112},{1,17},{17... | collective-permute-start | bytes 98312 | tf_op jit(solution)/shard_map/ppermute | solution.py:18
  50.2 1.3 collective-permute-start.5
  51.5 23.7 %all_gather.3 = bf16[27,128,64]{2,1,0:T(8,128)(2,1)S(1)} all-gather(bf16[27,8,64]{2,1,0:T(8,128)(2,1)S(1)} %copy-done.14), channel_id=1, replica_groups=mesh['depth'=8,'height'=16] {'height'}, dimensions={1}, use_global_device_ids=true | all-gather | bytes 470016 | tf_op jit(solution)/shard_map/all_gather | solution.py:120
  75.2 2.3 collective-permute-start.6
  77.5 5.7 %collective-permute-start.7 = (bf16[64,4,1,64]{0,3,2,1:T(8,128)(2,1)S(1)}, bf16[64,4,1,64]{0,3,2,1:T(8,128)(2,1)S(1)}, u32[]{:S(2)}, u32[]{:S(2)}) collective-permute-start(bf16[64,4,1,64]{0,3,2,1:T(8,128)(2,1)S(1)} %get-tuple-element.25), channel_id=1, source_target_pairs={{1,0},{2,1},{3,2},{4,3},{5,4},{6,5},{7,6},{8,7},{9,8},{10,9},{11,1... | collective-permute-start | bytes 98312 | tf_op jit(solution)/shard_map/ppermute | solution.py:19
  83.4 1.7 collective-permute-done.7
  90.5 0.4 fusion.283
  96.6 4.0 %collective-permute-start.8 = (bf16[128,1,4,64]{0,3,2,1:T(8,128)(2,1)S(1)}, bf16[128,1,4,64]{0,3,2,1:T(8,128)(2,1)S(1)}, u32[]{:S(2)}, u32[]{:S(2)}) collective-permute-start(bf16[128,1,4,64]{0,3,2,1:T(8,128)(2,1)S(1)} %get-tuple-element.31), channel_id=1, source_target_pairs={{0,16},{16,32},{32,48},{48,64},{64,80},{80,96},{96,112},{1,17},{17... | collective-permute-start | bytes 196616 | tf_op jit(solution)/shard_map/ppermute | solution.py:18
  100.5 1.3 collective-permute-start.9
  102.0 0.9 collective-permute-done.8
  102.9 4.1 %collective-permute-done.9 = bf16[128,1,4,64]{0,3,2,1:T(8,128)(2,1)S(1)} collective-permute-done((bf16[128,1,4,64]{0,3,2,1:T(8,128)(2,1)S(1)}, bf16[128,1,4,64]{0,3,2,1:T(8,128)(2,1)S(1)}, u32[]{:S(2)}, u32[]{:S(2)}) %collective-permute-start.9) | collective-permute-done | bytes 65568 | tf_op jit(solution)/shard_map/ppermute | solution.py:19
  107.1 4.9 %collective-permute-start.11 = (bf16[128,4,1,64]{0,3,2,1:T(8,128)(2,1)S(1)}, bf16[128,4,1,64]{0,3,2,1:T(8,128)(2,1)S(1)}, u32[]{:S(2)}, u32[]{:S(2)}) collective-permute-start(bf16[128,4,1,64]{0,3,2,1:T(8,128)(2,1)S(1)} %get-tuple-element.23), channel_id=1, source_target_pairs={{1,0},{2,1},{3,2},{4,3},{5,4},{6,5},{7,6},{8,7},{9,8},{10,9},{11,1... | collective-permute-start | bytes 196616 | tf_op jit(solution)/shard_map/ppermute | solution.py:19
  112.0 1.9 collective-permute-start.10
  114.2 5.8 %collective-permute-done.10 = bf16[128,4,1,64]{0,3,2,1:T(8,128)(2,1)S(1)} collective-permute-done((bf16[128,4,1,64]{0,3,2,1:T(8,128)(2,1)S(1)}, bf16[128,4,1,64]{0,3,2,1:T(8,128)(2,1)S(1)}, u32[]{:S(2)}, u32[]{:S(2)}) %collective-permute-start.10) | collective-permute-done | bytes 65568 | tf_op jit(solution)/shard_map/ppermute | solution.py:18
  125.1 0.4 broadcast_in_dim.10
  125.5 1.5 broadcast_in_dim.11
  127.0 2.2 copy.120
  129.2 1.9 fusion.210
  139.0 0.7 copy-done.12
  139.8 0.8 fusion.124
  140.7 3.3 copy.149
  144.3 1.3 collective-permute-start.13
  145.6 4.6 %collective-permute-start.12 = (bf16[64,1,8,128]{3,0,2,1:T(8,128)(2,1)S(1)}, bf16[64,1,8,128]{3,0,2,1:T(8,128)(2,1)S(1)}, u32[]{:S(2)}, u32[]{:S(2)}) collective-permute-start(bf16[64,1,8,128]{3,0,2,1:T(8,128)(2,1)S(1)} %get-tuple-element.16), channel_id=1, source_target_pairs={{0,16},{16,32},{32,48},{48,64},{64,80},{80,96},{96,112},{1,17},{17... | collective-permute-start | bytes 393224 | tf_op jit(solution)/shard_map/ppermute | solution.py:18
  150.1 134.6 %all-reduce.6.cloned.1.call-done = f32[27,64,32]{1,2,0:T(8,128)} async-done(((f32[27,64,32]{1,2,0:T(8,128)}), f32[27,64,32]{1,2,0:T(8,128)}) %all-reduce.6.cloned.1.call-update) | async-done | bytes 221200 | tf_op jit(solution)/shard_map/psum | solution.py:142
  284.7 1.8 broadcast_multiply_fusion
  286.6 1.9 collective-permute-start.14
  288.5 6.3 %collective-permute-start.15 = (bf16[64,6,1,128]{3,0,2,1:T(8,128)(2,1)S(1)}, bf16[64,6,1,128]{3,0,2,1:T(8,128)(2,1)S(1)}, u32[]{:S(2)}, u32[]{:S(2)}) collective-permute-start(bf16[64,6,1,128]{3,0,2,1:T(8,128)(2,1)S(1)} %get-tuple-element.15), channel_id=1, source_target_pairs={{1,0},{2,1},{3,2},{4,3},{5,4},{6,5},{7,6},{8,7},{9,8},{10,9},{11,1... | collective-permute-start | bytes 294920 | tf_op jit(solution)/shard_map/ppermute | solution.py:19
  295.2 1.5 collective-permute-done.15
  297.3 1.8 select_maximum_fusion
  299.7 0.4 fusion.236
  300.3 0.4 fusion.242
  300.9 0.4 fusion.248
  301.9 0.4 fusion.227
  302.9 0.4 convolution_bitcast_fusion.15
  303.5 0.4 convolution_bitcast_fusion.18
  304.4 0.7 fusion.52
  305.3 0.4 fusion.53
  305.8 0.8 copy.150
  306.6 33.3 %psum.16 = bf16[27,8,64]{2,0,1:T(8,128)(2,1)S(1)} all-reduce(bf16[27,8,64]{2,0,1:T(8,128)(2,1)} %reduce-scatter.2.cloned.1.call-done), channel_id=1, replica_groups=mesh['depth'=8,'height'=16] {'depth'}, use_global_device_ids=true, to_apply=%region_2.3 | all-reduce | flops 13824 | bytes 55296 | tf_op jit(solution)/shard_map/psum | solution.py:126
  339.9 0.7 copy.151
  (203 shorter events, 34.6 us)
Async XLA Ops:
  8.0 18.7 %copy-start = (bf16[32,4,8,128]{3,2,1,0:T(8,128)(2,1)S(1)}, bf16[32,4,8,128]{3,2,1,0:T(8,128)(2,1)}, u32[]{:S(2)}) copy-start(bf16[32,4,8,128]{3,2,1,0:T(8,128)(2,1)} %param.4) | copy-start | bytes 786436
  8.0 18.7 %copy-start.6 = (bf16[27,64,32]{1,2,0:T(8,128)(2,1)S(1)}, bf16[27,64,32]{1,2,0:T(8,128)(2,1)}, u32[]{:S(2)}) copy-start(bf16[27,64,32]{1,2,0:T(8,128)(2,1)} %param.5) | copy-start | bytes 331780
  8.0 276.7 %all-reduce.6.cloned.1.call-start = ((), (), s32[]{:S(2)}) async-start(), calls=%async_computation.1 | async-start | bytes 884736 | tf_op jit(solution)/shard_map/psum | solution.py:142
  9.0 5.4 %collective-permute-start = (bf16[32,1,8,128]{3,0,2,1:T(8,128)(2,1)S(1)}, bf16[32,1,8,128]{3,0,2,1:T(8,128)(2,1)S(1)}, u32[]{:S(2)}, u32[]{:S(2)}) collective-permute-start(bf16[32,1,8,128]{3,0,2,1:T(8,128)(2,1)S(1)} %copy.321), channel_id=1, source_target_pairs={{0,16},{16,32},{32,48},{48,64},{64,80},{80,96},{96,112},{1,17},{17... | collective-permute-start | bytes 196616 | tf_op jit(solution)/shard_map/ppermute | solution.py:18
  12.5 6.2 %collective-permute-start.1 = (bf16[32,1,8,128]{3,0,2,1:T(8,128)(2,1)S(1)}, bf16[32,1,8,128]{3,0,2,1:T(8,128)(2,1)S(1)}, u32[]{:S(2)}, u32[]{:S(2)}) collective-permute-start(bf16[32,1,8,128]{3,0,2,1:T(8,128)(2,1)S(1)} %copy.322), channel_id=1, source_target_pairs={{16,0},{32,16},{48,32},{64,48},{80,64},{96,80},{112,96},{17,1},{33... | collective-permute-start | bytes 196616 | tf_op jit(solution)/shard_map/ppermute | solution.py:19
  15.6 19.9 %copy-start.4 = (bf16[32,5,8,128]{3,0,2,1:T(8,128)(2,1)}, bf16[32,5,8,128]{3,0,2,1:T(8,128)(2,1)S(1)}, u32[]{:S(2)}) copy-start(bf16[32,5,8,128]{3,0,2,1:T(8,128)(2,1)S(1)} %get-tuple-element.28) | copy-start | bytes 983044
  18.7 19.6 %copy-start.2 = (bf16[32,5,8,128]{3,0,2,1:T(8,128)(2,1)}, bf16[32,5,8,128]{3,0,2,1:T(8,128)(2,1)S(1)}, u32[]{:S(2)}) copy-start(bf16[32,5,8,128]{3,0,2,1:T(8,128)(2,1)S(1)} %get-tuple-element.35) | copy-start | bytes 983044
  18.8 8.3 %collective-permute-start.2 = (bf16[32,6,1,128]{3,0,2,1:T(8,128)(2,1)S(1)}, bf16[32,6,1,128]{3,0,2,1:T(8,128)(2,1)S(1)}, u32[]{:S(2)}, u32[]{:S(2)}) collective-permute-start(bf16[32,6,1,128]{3,0,2,1:T(8,128)(2,1)S(1)} %get-tuple-element.18), channel_id=1, source_target_pairs={{0,1},{1,2},{2,3},{3,4},{4,5},{5,6},{6,7},{7,8},{8,9},{9,10},{10,1... | collective-permute-start | bytes 147464 | tf_op jit(solution)/shard_map/ppermute | solution.py:18
  20.7 7.8 %collective-permute-start.3 = (bf16[32,6,1,128]{3,0,2,1:T(8,128)(2,1)S(1)}, bf16[32,6,1,128]{3,0,2,1:T(8,128)(2,1)S(1)}, u32[]{:S(2)}, u32[]{:S(2)}) collective-permute-start(bf16[32,6,1,128]{3,0,2,1:T(8,128)(2,1)S(1)} %get-tuple-element.19), channel_id=1, source_target_pairs={{1,0},{2,1},{3,2},{4,3},{5,4},{6,5},{7,6},{8,7},{9,8},{10,9},{11,1... | collective-permute-start | bytes 147464 | tf_op jit(solution)/shard_map/ppermute | solution.py:19
  27.1 9.8 %copy-start.10 = (bf16[32,6,1,128]{3,0,2,1:T(8,128)(2,1)}, bf16[32,6,1,128]{3,0,2,1:T(8,128)(2,1)S(1)}, u32[]{:S(2)}) copy-start(bf16[32,6,1,128]{3,0,2,1:T(8,128)(2,1)S(1)} %collective-permute-done.2) | copy-start | bytes 147460
  28.5 9.5 %copy-start.8 = (bf16[32,6,1,128]{3,0,2,1:T(8,128)(2,1)}, bf16[32,6,1,128]{3,0,2,1:T(8,128)(2,1)S(1)}, u32[]{:S(2)}) copy-start(bf16[32,6,1,128]{3,0,2,1:T(8,128)(2,1)S(1)} %collective-permute-done.3) | copy-start | bytes 147460
  42.2 9.3 %copy-start.14 = (bf16[27,8,64]{2,1,0:T(8,128)(2,1)S(1)}, bf16[27,8,64]{2,1,0:T(8,128)(2,1)}, u32[]{:S(2)}) copy-start(bf16[27,8,64]{2,1,0:T(8,128)(2,1)} %param.6) | copy-start | bytes 82948
  45.6 29.6 %collective-permute-start.4 = (bf16[64,1,4,64]{0,3,2,1:T(8,128)(2,1)S(1)}, bf16[64,1,4,64]{0,3,2,1:T(8,128)(2,1)S(1)}, u32[]{:S(2)}, u32[]{:S(2)}) collective-permute-start(bf16[64,1,4,64]{0,3,2,1:T(8,128)(2,1)S(1)} %get-tuple-element.33), channel_id=1, source_target_pairs={{0,16},{16,32},{32,48},{48,64},{64,80},{80,96},{96,112},{1,17},{17... | collective-permute-start | bytes 98312 | tf_op jit(solution)/shard_map/ppermute | solution.py:18
  50.2 25.0 %collective-permute-start.5 = (bf16[64,1,4,64]{0,3,2,1:T(8,128)(2,1)S(1)}, bf16[64,1,4,64]{0,3,2,1:T(8,128)(2,1)S(1)}, u32[]{:S(2)}, u32[]{:S(2)}) collective-permute-start(bf16[64,1,4,64]{0,3,2,1:T(8,128)(2,1)S(1)} %get-tuple-element.34), channel_id=1, source_target_pairs={{16,0},{32,16},{48,32},{64,48},{80,64},{96,80},{112,96},{17,1},{33... | collective-permute-start | bytes 98312 | tf_op jit(solution)/shard_map/ppermute | solution.py:19
  75.2 8.2 %collective-permute-start.6 = (bf16[64,4,1,64]{0,3,2,1:T(8,128)(2,1)S(1)}, bf16[64,4,1,64]{0,3,2,1:T(8,128)(2,1)S(1)}, u32[]{:S(2)}, u32[]{:S(2)}) collective-permute-start(bf16[64,4,1,64]{0,3,2,1:T(8,128)(2,1)S(1)} %get-tuple-element.24), channel_id=1, source_target_pairs={{0,1},{1,2},{2,3},{3,4},{4,5},{5,6},{6,7},{7,8},{8,9},{9,10},{10,1... | collective-permute-start | bytes 98312 | tf_op jit(solution)/shard_map/ppermute | solution.py:18
  77.5 7.6 %collective-permute-start.7 = (bf16[64,4,1,64]{0,3,2,1:T(8,128)(2,1)S(1)}, bf16[64,4,1,64]{0,3,2,1:T(8,128)(2,1)S(1)}, u32[]{:S(2)}, u32[]{:S(2)}) collective-permute-start(bf16[64,4,1,64]{0,3,2,1:T(8,128)(2,1)S(1)} %get-tuple-element.25), channel_id=1, source_target_pairs={{1,0},{2,1},{3,2},{4,3},{5,4},{6,5},{7,6},{8,7},{9,8},{10,9},{11,1... | collective-permute-start | bytes 98312 | tf_op jit(solution)/shard_map/ppermute | solution.py:19
  89.6 0.9 copy-start.15
  96.6 6.4 %collective-permute-start.8 = (bf16[128,1,4,64]{0,3,2,1:T(8,128)(2,1)S(1)}, bf16[128,1,4,64]{0,3,2,1:T(8,128)(2,1)S(1)}, u32[]{:S(2)}, u32[]{:S(2)}) collective-permute-start(bf16[128,1,4,64]{0,3,2,1:T(8,128)(2,1)S(1)} %get-tuple-element.31), channel_id=1, source_target_pairs={{0,16},{16,32},{32,48},{48,64},{64,80},{80,96},{96,112},{1,17},{17... | collective-permute-start | bytes 196616 | tf_op jit(solution)/shard_map/ppermute | solution.py:18
  100.5 6.5 %collective-permute-start.9 = (bf16[128,1,4,64]{0,3,2,1:T(8,128)(2,1)S(1)}, bf16[128,1,4,64]{0,3,2,1:T(8,128)(2,1)S(1)}, u32[]{:S(2)}, u32[]{:S(2)}) collective-permute-start(bf16[128,1,4,64]{0,3,2,1:T(8,128)(2,1)S(1)} %get-tuple-element.32), channel_id=1, source_target_pairs={{16,0},{32,16},{48,32},{64,48},{80,64},{96,80},{112,96},{17,1},{33... | collective-permute-start | bytes 196616 | tf_op jit(solution)/shard_map/ppermute | solution.py:19
  107.1 7.1 %collective-permute-start.11 = (bf16[128,4,1,64]{0,3,2,1:T(8,128)(2,1)S(1)}, bf16[128,4,1,64]{0,3,2,1:T(8,128)(2,1)S(1)}, u32[]{:S(2)}, u32[]{:S(2)}) collective-permute-start(bf16[128,4,1,64]{0,3,2,1:T(8,128)(2,1)S(1)} %get-tuple-element.23), channel_id=1, source_target_pairs={{1,0},{2,1},{3,2},{4,3},{5,4},{6,5},{7,6},{8,7},{9,8},{10,9},{11,1... | collective-permute-start | bytes 196616 | tf_op jit(solution)/shard_map/ppermute | solution.py:19
  112.0 8.0 %collective-permute-start.10 = (bf16[128,4,1,64]{0,3,2,1:T(8,128)(2,1)S(1)}, bf16[128,4,1,64]{0,3,2,1:T(8,128)(2,1)S(1)}, u32[]{:S(2)}, u32[]{:S(2)}) collective-permute-start(bf16[128,4,1,64]{0,3,2,1:T(8,128)(2,1)S(1)} %get-tuple-element.22), channel_id=1, source_target_pairs={{0,1},{1,2},{2,3},{3,4},{4,5},{5,6},{6,7},{7,8},{8,9},{9,10},{10,1... | collective-permute-start | bytes 196616 | tf_op jit(solution)/shard_map/ppermute | solution.py:18
  114.1 6.5 %copy-start.13 = (bf16[27,128,64]{1,2,0:T(8,128)(2,1)}, bf16[27,128,64]{1,2,0:T(8,128)(2,1)S(1)}, u32[]{:S(2)}) copy-start(bf16[27,128,64]{1,2,0:T(8,128)(2,1)S(1)} %fusion.126) | copy-start | bytes 1327108
  129.2 2.2 copy-start.11
  131.1 1.1 copy-start.5
  131.6 1.5 copy-start.9
  133.4 1.5 copy-start.1
  136.0 1.5 copy-start.3
  139.0 0.8 copy-start.12
  139.0 5.0 %copy-start.7 = (bf16[27,64,32]{1,2,0:T(8,128)(2,1)S(1)}, bf16[27,64,32]{1,2,0:T(8,128)(2,1)}, u32[]{:S(2)}) copy-start(bf16[27,64,32]{1,2,0:T(8,128)(2,1)} %param.5) | copy-start | bytes 331780
  139.8 166.8 %reduce-scatter.2.cloned.1.call-start = ((), (), s32[]{:S(2)}) async-start(), calls=%async_computation.2 | async-start | bytes 1114112 | tf_op jit(solution)/shard_map/reduce_scatter | solution.py:128
  144.3 142.3 %collective-permute-start.13 = (bf16[64,1,8,128]{3,0,2,1:T(8,128)(2,1)S(1)}, bf16[64,1,8,128]{3,0,2,1:T(8,128)(2,1)S(1)}, u32[]{:S(2)}, u32[]{:S(2)}) collective-permute-start(bf16[64,1,8,128]{3,0,2,1:T(8,128)(2,1)S(1)} %get-tuple-element.17), channel_id=1, source_target_pairs={{16,0},{32,16},{48,32},{64,48},{80,64},{96,80},{112,96},{17,1},{33... | collective-permute-start | bytes 393224 | tf_op jit(solution)/shard_map/ppermute | solution.py:19
  145.6 141.0 %collective-permute-start.12 = (bf16[64,1,8,128]{3,0,2,1:T(8,128)(2,1)S(1)}, bf16[64,1,8,128]{3,0,2,1:T(8,128)(2,1)S(1)}, u32[]{:S(2)}, u32[]{:S(2)}) collective-permute-start(bf16[64,1,8,128]{3,0,2,1:T(8,128)(2,1)S(1)} %get-tuple-element.16), channel_id=1, source_target_pairs={{0,16},{16,32},{32,48},{48,64},{64,80},{80,96},{96,112},{1,17},{17... | collective-permute-start | bytes 393224 | tf_op jit(solution)/shard_map/ppermute | solution.py:18
  286.6 8.6 %collective-permute-start.14 = (bf16[64,6,1,128]{3,0,2,1:T(8,128)(2,1)S(1)}, bf16[64,6,1,128]{3,0,2,1:T(8,128)(2,1)S(1)}, u32[]{:S(2)}, u32[]{:S(2)}) collective-permute-start(bf16[64,6,1,128]{3,0,2,1:T(8,128)(2,1)S(1)} %get-tuple-element.14), channel_id=1, source_target_pairs={{0,1},{1,2},{2,3},{3,4},{4,5},{5,6},{6,7},{7,8},{8,9},{9,10},{10,1... | collective-permute-start | bytes 294920 | tf_op jit(solution)/shard_map/ppermute | solution.py:18
  288.5 8.2 %collective-permute-start.15 = (bf16[64,6,1,128]{3,0,2,1:T(8,128)(2,1)S(1)}, bf16[64,6,1,128]{3,0,2,1:T(8,128)(2,1)S(1)}, u32[]{:S(2)}, u32[]{:S(2)}) collective-permute-start(bf16[64,6,1,128]{3,0,2,1:T(8,128)(2,1)S(1)} %get-tuple-element.15), channel_id=1, source_target_pairs={{1,0},{2,1},{3,2},{4,3},{5,4},{6,5},{7,6},{8,7},{9,8},{10,9},{11,1... | collective-permute-start | bytes 294920 | tf_op jit(solution)/shard_map/ppermute | solution.py:19
Sparse Core Ops, SparseCore 0:
  139.9 144.7 all-reduce.5
Sparse Core Ops, SparseCore 1:
  144.6 66.4 reduce-scatter.1
where the time goes:
time: 349 us; the launch traced here: 348 us
  waiting for transfers between devices  154 us (44%)
  blocking collectives  57 us (16%)
  starting transfers between devices  52.8 us (15%)
  matrix products  43.6 us (12%)
  between operations  16.6 us (5%)
  local copies, waits for them, and re-layouts  14.2 us (4%)
  other arithmetic  10.1 us (3%)
    psum x1, waiting for transfers between devices, shards(): grad_three = lax.psum(partial_three, ('depth', 'height')) * scale_three  135 us
    psum x1, blocking collectives, shards(): depth_summed = lax.psum(partial_four.astype(jnp.bfloat16), 'depth')  33.3 us
    ppermute x8, starting transfers between devices, extended_2(): after = lax.ppermute(first, axis, down)  28.1 us
    ppermute x8, starting transfers between devices, extended_2(): before = lax.ppermute(last, axis, up)  24.6 us
    all_gather x1, blocking collectives, shards(): full_bank = lax.all_gather(filters_four, 'height', axis=1, tiled=True)  23.7 us
    dot_general x54, matrix products, forward_taps(): jnp.einsum('oi,idhw->odhw', weights[9 * first + 3 * second + third], wind...  16.9 us
    dot_general x54, matrix products, weight_taps(): jnp.einsum('odhw,idhw->oi', delta, window_piece, preferred_element_type=j...  14.4 us
    dot_general x54, matrix products, transpose_taps(): jnp.einsum('oi,odhw->idhw', weights[9 * first + 3 * second + third], wind...  12.3 us
  transfers between devices with their start and end apart: 18, of which 9 were waited for; matrix products, arithmetic and copies ran while one was open for 5% of the time, Pallas kernels for 0%

commit v1 on v0

--- a/solution.py
+++ b/solution.py
@@ -139,7 +139,7 @@
     )
     delta_three = (spread * gelu_slope(act_three)).astype(jnp.bfloat16)
     partial_three = weight_taps(delta_three, padded, depth_cells, height_cells, width_cells)
-    grad_three = lax.psum(partial_three, ("depth", "height")) * scale_three
+    grad_three = jnp.sum(lax.all_gather(partial_three, ("depth", "height")), axis=0) * scale_three
     delta_extended = extended_2(delta_three, (("depth", 1), ("height", 2)), 1)
     grad_volume = transpose_taps(
         pad_width(delta_extended), filters_three, depth_cells, height_cells, width_cells

time: 349 us -> 487 us (1.40)
  waiting for transfers between devices: 154 us -> 272 us
  other arithmetic: 10.1 us -> 28.1 us
    all_gather x0 -> x1, waiting for transfers between devices: none -> 224 us  [shards(): lax.all_gather(partial_three, ('depth', 'height'))]
    psum x1 -> x0, waiting for transfers between devices: 135 us -> none  [shards(): grad_three = lax.psum(partial_three, ('depth', 'height')) * scale_three]
    reduce_scatter x1, waiting for transfers between devices: 0.01 us -> 27.2 us  [shards(): lax.psum_scatter(depth_summed, 'height', scatter_dimension=1, tiled=True)]
    reduce_sum x0 -> x1, other arithmetic: none -> 18.1 us  [shards(): jnp.sum(lax.all_gather(partial_three, ('depth', 'height')), axis=0)]
  transfers between devices with their start and end apart: 18 -> 18, of which waited for: 9 -> 13; matrix products, arithmetic and copies ran while one was open for 5% -> 7% of each run, Pallas kernels for 0% -> 0%
where the time goes in v1:
time: 487 us; the launch traced here: 486 us
  waiting for transfers between devices  272 us (56%)
  blocking collectives  61.6 us (13%)
  starting transfers between devices  53 us (11%)
  matrix products  43.1 us (9%)
  other arithmetic  28.1 us (6%)
  between operations  16.6 us (3%)
  local copies, waits for them, and re-layouts  11.4 us (2%)
    all_gather x1, waiting for transfers between devices, shards(): lax.all_gather(partial_three, ('depth', 'height'))  224 us
    psum x1, blocking collectives, shards(): depth_summed = lax.psum(partial_four.astype(jnp.bfloat16), 'depth')  37.7 us
    ppermute x8, starting transfers between devices, extended_2(): after = lax.ppermute(first, axis, down)  28.1 us
    reduce_scatter x1, waiting for transfers between devices, shards(): lax.psum_scatter(depth_summed, 'height', scatter_dimension=1, tiled=True)  27.2 us
    ppermute x8, starting transfers between devices, extended_2(): before = lax.ppermute(last, axis, up)  24.6 us
    all_gather x1, blocking collectives, shards(): full_bank = lax.all_gather(filters_four, 'height', axis=1, tiled=True)  23.9 us
    reduce_sum x1, other arithmetic, shards(): jnp.sum(lax.all_gather(partial_three, ('depth', 'height')), axis=0)  18.1 us
    dot_general x54, matrix products, forward_taps(): jnp.einsum('oi,idhw->odhw', weights[9 * first + 3 * second + third], wind...  17.1 us
  transfers between devices with their start and end apart: 18, of which 13 were waited for; matrix products, arithmetic and copies ran while one was open for 7% of the time, Pallas kernels for 0%

profile of v1, /device:TPU:6, one launch (start us, length us, event | category | flops | bytes accessed | tf_op | source)
XLA Modules:
  0.0 485.7 jit_solution(8380752418296855722)
XLA Ops:
  8.1 0.9 fusion.559
  9.0 3.5 collective-permute-start
  12.5 1.3 collective-permute-start.1
  13.8 0.6 collective-permute-done
  14.4 1.2 constant_dynamic-update-slice_fusion.6
  15.6 3.1 collective-permute-done.1
  18.8 1.9 collective-permute-start.2
  20.7 6.0 %collective-permute-start.3 = (bf16[32,6,1,128]{3,0,2,1:T(8,128)(2,1)S(1)}, bf16[32,6,1,128]{3,0,2,1:T(8,128)(2,1)S(1)}, u32[]{:S(2)}, u32[]{:S(2)}) collective-permute-start(bf16[32,6,1,128]{3,0,2,1:T(8,128)(2,1)S(1)} %get-tuple-element.19), channel_id=1, source_target_pairs={{1,0},{2,1},{3,2},{4,3},{5,4},{6,5},{7,6},{8,7},{9,8},{10,9},{11,1... | collective-permute-start | bytes 147464 | tf_op jit(solution)/shard_map/ppermute | solution.py:19
  27.1 1.4 collective-permute-done.3
  28.5 0.5 fusion.212
  29.3 0.4 fusion.320
  30.0 0.4 fusion.314
  30.7 0.4 fusion.308
  31.1 0.4 convolution_bitcast_fusion.10
  32.2 0.4 convolution_bitcast_fusion.8
  32.9 0.4 convolution_bitcast_fusion.4
  33.7 0.4 convolution_bitcast_fusion.6
  34.7 0.4 convolution_add_fusion.4
  36.5 0.5 fusion.24
  37.0 0.4 fusion.22
  37.4 0.7 fusion.27
  38.5 2.1 add_multiply_fusion
  40.6 1.8 copy.91
  42.4 2.4 reduce_sum.18
  44.9 1.0 multiply_convert_fusion
  45.8 4.6 collective-permute-start.4
  50.5 1.3 collective-permute-start.5
  51.8 23.9 %all_gather.9 = bf16[27,128,64]{2,1,0:T(8,128)(2,1)S(1)} all-gather(bf16[27,8,64]{2,1,0:T(8,128)(2,1)} %param.6), channel_id=1, replica_groups=mesh['depth'=8,'height'=16] {'height'}, dimensions={1}, use_global_device_ids=true | all-gather | bytes 470016 | tf_op jit(solution)/shard_map/all_gather | solution.py:120
  75.7 2.3 collective-permute-start.6
  78.0 5.7 %collective-permute-start.7 = (bf16[64,4,1,64]{0,3,2,1:T(8,128)(2,1)S(1)}, bf16[64,4,1,64]{0,3,2,1:T(8,128)(2,1)S(1)}, u32[]{:S(2)}, u32[]{:S(2)}) collective-permute-start(bf16[64,4,1,64]{0,3,2,1:T(8,128)(2,1)S(1)} %get-tuple-element.25), channel_id=1, source_target_pairs={{1,0},{2,1},{3,2},{4,3},{5,4},{6,5},{7,6},{8,7},{9,8},{10,9},{11,1... | collective-permute-start | bytes 98312 | tf_op jit(solution)/shard_map/ppermute | solution.py:19
  83.9 1.7 collective-permute-done.7
  91.0 0.4 fusion.283
  97.2 4.0 collective-permute-start.8
  101.2 1.3 collective-permute-start.9
  102.7 0.9 collective-permute-done.8
  103.6 4.1 collective-permute-done.9
  107.7 0.6 pad_maximum_fusion.20
  108.4 4.9 %collective-permute-start.11 = (bf16[128,4,1,64]{0,3,2,1:T(8,128)(2,1)}, bf16[128,4,1,64]{0,3,2,1:T(8,128)(2,1)S(1)}, u32[]{:S(2)}, u32[]{:S(2)}) collective-permute-start(bf16[128,4,1,64]{0,3,2,1:T(8,128)(2,1)} %get-tuple-element.23), channel_id=1, source_target_pairs={{1,0},{2,1},{3,2},{4,3},{5,4},{6,5},{7,6},{8,7},{9,8},{10,9},{11,1... | collective-permute-start | bytes 196616 | tf_op jit(solution)/shard_map/ppermute | solution.py:19
  113.3 1.9 collective-permute-start.10
  115.4 2.5 copy.149
  118.2 3.1 collective-permute-done.10
  126.4 0.4 broadcast_in_dim.10
  126.9 1.6 copy.120
  128.5 2.3 fusion.210
  138.6 0.8 copy-done.10
  139.4 1.3 collective-permute-start.13
  140.7 4.6 collective-permute-start.12
  145.5 1.4 collective-permute-done.13
  146.9 0.9 collective-permute-done.12
  147.8 1.9 collective-permute-start.14
  149.8 6.3 %collective-permute-start.15 = (bf16[64,6,1,128]{3,0,2,1:T(8,128)(2,1)S(1)}, bf16[64,6,1,128]{3,0,2,1:T(8,128)(2,1)S(1)}, u32[]{:S(2)}, u32[]{:S(2)}) collective-permute-start(bf16[64,6,1,128]{3,0,2,1:T(8,128)(2,1)S(1)} %get-tuple-element.15), channel_id=1, source_target_pairs={{1,0},{2,1},{3,2},{4,3},{5,4},{6,5},{7,6},{8,7},{9,8},{10,9},{11,1... | collective-permute-start | bytes 294920 | tf_op jit(solution)/shard_map/ppermute | solution.py:19
  156.5 1.8 collective-permute-done.14
  158.3 1.8 collective-permute-done.15
  160.6 1.8 select_maximum_fusion
  166.7 0.4 convolution_bitcast_fusion.18
  167.7 0.6 fusion.52
  168.5 0.4 fusion.53
  168.9 0.8 copy.150
  169.7 27.2 %reduce-scatter.2.cloned.1.call-done = bf16[27,8,64]{2,0,1:T(8,128)(2,1)} async-done(((bf16[27,128,64]{2,0,1:T(8,128)(2,1)}), bf16[27,8,64]{2,0,1:T(8,128)(2,1)}) %reduce-scatter.2.cloned.1.call-update) | async-done | bytes 27664 | tf_op jit(solution)/shard_map/reduce_scatter | solution.py:128
  197.0 37.7 %psum.8 = bf16[27,8,64]{2,0,1:T(8,128)(2,1)S(1)} all-reduce(bf16[27,8,64]{2,0,1:T(8,128)(2,1)} %reduce-scatter.2.cloned.1.call-done), channel_id=1, replica_groups=mesh['depth'=8,'height'=16] {'depth'}, use_global_device_ids=true, to_apply=%region_2.3 | all-reduce | flops 13824 | bytes 55296 | tf_op jit(solution)/shard_map/psum | solution.py:126
  234.7 0.7 copy.151
  235.4 223.9 %all-gather.3.cloned.1.call-done = f32[3456,64,32]{1,2,0:T(8,128)} async-done(((f32[27,64,32]{1,2,0:T(8,128)}), f32[3456,64,32]{1,2,0:T(8,128)}) %all-gather.3.cloned.1.call-update) | async-done | bytes 28311568 | tf_op jit(solution)/shard_map/all_gather | solution.py:142
  459.4 18.1 %reduce_sum.19 = f32[27,64,32]{1,2,0:T(8,128)S(1)} reduce(f32[128,27,64,32]{2,3,1,0:T(8,128)} %bitcast.1362, f32[]{:T(128)} %constant.15.clone.1), dimensions={0}, to_apply=%region_1.2 | reduce | flops 7022592 | bytes 28532740 | tf_op jit(solution)/shard_map/reduce_sum | solution.py:142
  477.5 0.8 broadcast_multiply_fusion
  (196 shorter events, 36.5 us)
Async XLA Ops:
  8.0 18.7 %copy-start = (bf16[32,4,8,128]{3,2,1,0:T(8,128)(2,1)S(1)}, bf16[32,4,8,128]{3,2,1,0:T(8,128)(2,1)}, u32[]{:S(2)}) copy-start(bf16[32,4,8,128]{3,2,1,0:T(8,128)(2,1)} %param.4) | copy-start | bytes 786436
  8.0 18.7 %copy-start.6 = (bf16[27,64,32]{1,2,0:T(8,128)(2,1)S(1)}, bf16[27,64,32]{1,2,0:T(8,128)(2,1)}, u32[]{:S(2)}) copy-start(bf16[27,64,32]{1,2,0:T(8,128)(2,1)} %param.5) | copy-start | bytes 331780
  8.0 188.9 %reduce-scatter.2.cloned.1.call-start = ((), (), s32[]{:S(2)}) async-start(), calls=%async_computation.2 | async-start | bytes 1114112 | tf_op jit(solution)/shard_map/reduce_scatter | solution.py:128
  9.0 5.4 %collective-permute-start = (bf16[32,1,8,128]{3,0,2,1:T(8,128)(2,1)S(1)}, bf16[32,1,8,128]{3,0,2,1:T(8,128)(2,1)S(1)}, u32[]{:S(2)}, u32[]{:S(2)}) collective-permute-start(bf16[32,1,8,128]{3,0,2,1:T(8,128)(2,1)S(1)} %copy.321), channel_id=1, source_target_pairs={{0,16},{16,32},{32,48},{48,64},{64,80},{80,96},{96,112},{1,17},{17... | collective-permute-start | bytes 196616 | tf_op jit(solution)/shard_map/ppermute | solution.py:18
  12.5 6.2 %collective-permute-start.1 = (bf16[32,1,8,128]{3,0,2,1:T(8,128)(2,1)S(1)}, bf16[32,1,8,128]{3,0,2,1:T(8,128)(2,1)S(1)}, u32[]{:S(2)}, u32[]{:S(2)}) collective-permute-start(bf16[32,1,8,128]{3,0,2,1:T(8,128)(2,1)S(1)} %copy.322), channel_id=1, source_target_pairs={{16,0},{32,16},{48,32},{64,48},{80,64},{96,80},{112,96},{17,1},{33... | collective-permute-start | bytes 196616 | tf_op jit(solution)/shard_map/ppermute | solution.py:19
  15.6 19.9 %copy-start.4 = (bf16[32,5,8,128]{3,0,2,1:T(8,128)(2,1)}, bf16[32,5,8,128]{3,0,2,1:T(8,128)(2,1)S(1)}, u32[]{:S(2)}) copy-start(bf16[32,5,8,128]{3,0,2,1:T(8,128)(2,1)S(1)} %get-tuple-element.28) | copy-start | bytes 983044
  18.7 19.8 %copy-start.2 = (bf16[32,5,8,128]{3,0,2,1:T(8,128)(2,1)}, bf16[32,5,8,128]{3,0,2,1:T(8,128)(2,1)S(1)}, u32[]{:S(2)}) copy-start(bf16[32,5,8,128]{3,0,2,1:T(8,128)(2,1)S(1)} %get-tuple-element.35) | copy-start | bytes 983044
  18.8 8.3 %collective-permute-start.2 = (bf16[32,6,1,128]{3,0,2,1:T(8,128)(2,1)S(1)}, bf16[32,6,1,128]{3,0,2,1:T(8,128)(2,1)S(1)}, u32[]{:S(2)}, u32[]{:S(2)}) collective-permute-start(bf16[32,6,1,128]{3,0,2,1:T(8,128)(2,1)S(1)} %get-tuple-element.18), channel_id=1, source_target_pairs={{0,1},{1,2},{2,3},{3,4},{4,5},{5,6},{6,7},{7,8},{8,9},{9,10},{10,1... | collective-permute-start | bytes 147464 | tf_op jit(solution)/shard_map/ppermute | solution.py:18
  20.7 7.8 %collective-permute-start.3 = (bf16[32,6,1,128]{3,0,2,1:T(8,128)(2,1)S(1)}, bf16[32,6,1,128]{3,0,2,1:T(8,128)(2,1)S(1)}, u32[]{:S(2)}, u32[]{:S(2)}) collective-permute-start(bf16[32,6,1,128]{3,0,2,1:T(8,128)(2,1)S(1)} %get-tuple-element.19), channel_id=1, source_target_pairs={{1,0},{2,1},{3,2},{4,3},{5,4},{6,5},{7,6},{8,7},{9,8},{10,9},{11,1... | collective-permute-start | bytes 147464 | tf_op jit(solution)/shard_map/ppermute | solution.py:19
  27.1 9.9 %copy-start.8 = (bf16[32,6,1,128]{3,0,2,1:T(8,128)(2,1)}, bf16[32,6,1,128]{3,0,2,1:T(8,128)(2,1)S(1)}, u32[]{:S(2)}) copy-start(bf16[32,6,1,128]{3,0,2,1:T(8,128)(2,1)S(1)} %collective-permute-done.2) | copy-start | bytes 147460
  45.8 29.8 %collective-permute-start.4 = (bf16[64,1,4,64]{0,3,2,1:T(8,128)(2,1)S(1)}, bf16[64,1,4,64]{0,3,2,1:T(8,128)(2,1)S(1)}, u32[]{:S(2)}, u32[]{:S(2)}) collective-permute-start(bf16[64,1,4,64]{0,3,2,1:T(8,128)(2,1)S(1)} %get-tuple-element.33), channel_id=1, source_target_pairs={{0,16},{16,32},{32,48},{48,64},{64,80},{80,96},{96,112},{1,17},{17... | collective-permute-start | bytes 98312 | tf_op jit(solution)/shard_map/ppermute | solution.py:18
  50.5 25.2 %collective-permute-start.5 = (bf16[64,1,4,64]{0,3,2,1:T(8,128)(2,1)S(1)}, bf16[64,1,4,64]{0,3,2,1:T(8,128)(2,1)S(1)}, u32[]{:S(2)}, u32[]{:S(2)}) collective-permute-start(bf16[64,1,4,64]{0,3,2,1:T(8,128)(2,1)S(1)} %get-tuple-element.34), channel_id=1, source_target_pairs={{16,0},{32,16},{48,32},{64,48},{80,64},{96,80},{112,96},{17,1},{33... | collective-permute-start | bytes 98312 | tf_op jit(solution)/shard_map/ppermute | solution.py:19
  75.7 8.2 %collective-permute-start.6 = (bf16[64,4,1,64]{0,3,2,1:T(8,128)(2,1)S(1)}, bf16[64,4,1,64]{0,3,2,1:T(8,128)(2,1)S(1)}, u32[]{:S(2)}, u32[]{:S(2)}) collective-permute-start(bf16[64,4,1,64]{0,3,2,1:T(8,128)(2,1)S(1)} %get-tuple-element.24), channel_id=1, source_target_pairs={{0,1},{1,2},{2,3},{3,4},{4,5},{5,6},{6,7},{7,8},{8,9},{9,10},{10,1... | collective-permute-start | bytes 98312 | tf_op jit(solution)/shard_map/ppermute | solution.py:18
  78.0 7.6 %collective-permute-start.7 = (bf16[64,4,1,64]{0,3,2,1:T(8,128)(2,1)S(1)}, bf16[64,4,1,64]{0,3,2,1:T(8,128)(2,1)S(1)}, u32[]{:S(2)}, u32[]{:S(2)}) collective-permute-start(bf16[64,4,1,64]{0,3,2,1:T(8,128)(2,1)S(1)} %get-tuple-element.25), channel_id=1, source_target_pairs={{1,0},{2,1},{3,2},{4,3},{5,4},{6,5},{7,6},{8,7},{9,8},{10,9},{11,1... | collective-permute-start | bytes 98312 | tf_op jit(solution)/shard_map/ppermute | solution.py:19
  90.1 0.9 copy-start.11
  97.2 6.4 %collective-permute-start.8 = (bf16[128,1,4,64]{0,3,2,1:T(8,128)(2,1)S(1)}, bf16[128,1,4,64]{0,3,2,1:T(8,128)(2,1)S(1)}, u32[]{:S(2)}, u32[]{:S(2)}) collective-permute-start(bf16[128,1,4,64]{0,3,2,1:T(8,128)(2,1)S(1)} %get-tuple-element.31), channel_id=1, source_target_pairs={{0,16},{16,32},{32,48},{48,64},{64,80},{80,96},{96,112},{1,17},{17... | collective-permute-start | bytes 196616 | tf_op jit(solution)/shard_map/ppermute | solution.py:18
  101.2 6.5 %collective-permute-start.9 = (bf16[128,1,4,64]{0,3,2,1:T(8,128)(2,1)S(1)}, bf16[128,1,4,64]{0,3,2,1:T(8,128)(2,1)S(1)}, u32[]{:S(2)}, u32[]{:S(2)}) collective-permute-start(bf16[128,1,4,64]{0,3,2,1:T(8,128)(2,1)S(1)} %get-tuple-element.32), channel_id=1, source_target_pairs={{16,0},{32,16},{48,32},{64,48},{80,64},{96,80},{112,96},{17,1},{33... | collective-permute-start | bytes 196616 | tf_op jit(solution)/shard_map/ppermute | solution.py:19
  108.4 9.8 %collective-permute-start.11 = (bf16[128,4,1,64]{0,3,2,1:T(8,128)(2,1)}, bf16[128,4,1,64]{0,3,2,1:T(8,128)(2,1)S(1)}, u32[]{:S(2)}, u32[]{:S(2)}) collective-permute-start(bf16[128,4,1,64]{0,3,2,1:T(8,128)(2,1)} %get-tuple-element.23), channel_id=1, source_target_pairs={{1,0},{2,1},{3,2},{4,3},{5,4},{6,5},{7,6},{8,7},{9,8},{10,9},{11,1... | collective-permute-start | bytes 196616 | tf_op jit(solution)/shard_map/ppermute | solution.py:19
  113.3 8.0 %collective-permute-start.10 = (bf16[128,4,1,64]{0,3,2,1:T(8,128)(2,1)S(1)}, bf16[128,4,1,64]{0,3,2,1:T(8,128)(2,1)S(1)}, u32[]{:S(2)}, u32[]{:S(2)}) collective-permute-start(bf16[128,4,1,64]{0,3,2,1:T(8,128)(2,1)S(1)} %get-tuple-element.22), channel_id=1, source_target_pairs={{0,1},{1,2},{2,3},{3,4},{4,5},{5,6},{6,7},{7,8},{8,9},{9,10},{10,1... | collective-permute-start | bytes 196616 | tf_op jit(solution)/shard_map/ppermute | solution.py:18
  117.9 341.4 %all-gather.3.cloned.1.call-start = ((), (), s32[]{:S(2)}) async-start(), calls=%async_computation.1 | async-start | bytes 57065472 | tf_op jit(solution)/shard_map/all_gather | solution.py:142
  128.5 2.5 copy-start.9
  130.7 1.1 copy-start.5
  133.0 1.5 copy-start.1
  135.7 1.5 copy-start.3
  137.7 7.6 %copy-start.7 = (bf16[27,64,32]{1,2,0:T(8,128)(2,1)S(1)}, bf16[27,64,32]{1,2,0:T(8,128)(2,1)}, u32[]{:S(2)}) copy-start(bf16[27,64,32]{1,2,0:T(8,128)(2,1)} %param.5) | copy-start | bytes 331780
  138.6 0.8 copy-start.10
  139.4 7.5 %collective-permute-start.13 = (bf16[64,1,8,128]{3,0,2,1:T(8,128)(2,1)S(1)}, bf16[64,1,8,128]{3,0,2,1:T(8,128)(2,1)S(1)}, u32[]{:S(2)}, u32[]{:S(2)}) collective-permute-start(bf16[64,1,8,128]{3,0,2,1:T(8,128)(2,1)S(1)} %get-tuple-element.17), channel_id=1, source_target_pairs={{16,0},{32,16},{48,32},{64,48},{80,64},{96,80},{112,96},{17,1},{33... | collective-permute-start | bytes 393224 | tf_op jit(solution)/shard_map/ppermute | solution.py:19
  140.7 7.1 %collective-permute-start.12 = (bf16[64,1,8,128]{3,0,2,1:T(8,128)(2,1)S(1)}, bf16[64,1,8,128]{3,0,2,1:T(8,128)(2,1)S(1)}, u32[]{:S(2)}, u32[]{:S(2)}) collective-permute-start(bf16[64,1,8,128]{3,0,2,1:T(8,128)(2,1)S(1)} %get-tuple-element.16), channel_id=1, source_target_pairs={{0,16},{16,32},{32,48},{48,64},{64,80},{80,96},{96,112},{1,17},{17... | collective-permute-start | bytes 393224 | tf_op jit(solution)/shard_map/ppermute | solution.py:18
  147.8 10.4 %collective-permute-start.14 = (bf16[64,6,1,128]{3,0,2,1:T(8,128)(2,1)S(1)}, bf16[64,6,1,128]{3,0,2,1:T(8,128)(2,1)S(1)}, u32[]{:S(2)}, u32[]{:S(2)}) collective-permute-start(bf16[64,6,1,128]{3,0,2,1:T(8,128)(2,1)S(1)} %get-tuple-element.14), channel_id=1, source_target_pairs={{0,1},{1,2},{2,3},{3,4},{4,5},{5,6},{6,7},{7,8},{8,9},{9,10},{10,1... | collective-permute-start | bytes 294920 | tf_op jit(solution)/shard_map/ppermute | solution.py:18
  149.8 10.2 %collective-permute-start.15 = (bf16[64,6,1,128]{3,0,2,1:T(8,128)(2,1)S(1)}, bf16[64,6,1,128]{3,0,2,1:T(8,128)(2,1)S(1)}, u32[]{:S(2)}, u32[]{:S(2)}) collective-permute-start(bf16[64,6,1,128]{3,0,2,1:T(8,128)(2,1)S(1)} %get-tuple-element.15), channel_id=1, source_target_pairs={{1,0},{2,1},{3,2},{4,3},{5,4},{6,5},{7,6},{8,7},{9,8},{10,9},{11,1... | collective-permute-start | bytes 294920 | tf_op jit(solution)/shard_map/ppermute | solution.py:19
Sparse Core Ops, SparseCore 0:
  118.1 78.8 reduce-scatter.1
Sparse Core Ops, SparseCore 1:
  139.5 319.8 all-gather.2
